TPU v7x, 32 devices: a whole 2x2x4 slice. The times are simulated.
32 devices in a mesh: rig: 2 (over y), row: 4 (over z), col: 4 (over x, core).
Axes of the slice: x: 2, y: 2, z: 4, core: 2. Of those that a mesh axis runs over, the one named last changes fastest.
Arguments:
- jacobian: bfloat16 [8, 4, 64, 64, 1024], P(('rig', 'row'), 'col'), parts along dimension 0, may hold values from -0.375 to 0.375
- block_rows: int32 [8, 4, 1024], P(('rig', 'row'), 'col'), parts along dimension 0, may hold values from 0 to 511
- block_cols: int32 [8, 4, 1024], P(('rig', 'row'), 'col'), parts along dimension 0, may hold values from 0 to 511
- counts: int32 [8, 4], P(('rig', 'row'), 'col'), parts along dimension 0, may hold values from 128 to 1024, as said below
- residuals: float32 [64, 4096], P(None, ('rig', 'row')), parts along dimension 1, may hold values from -6 to 6
- damping: float32 [64, 4096], P(None, ('rig', 'col')), parts along dimension 1, may hold values from 0.5 to 2
Outputs:
- step_field: float32 [64, 4096], P(None, ('rig', 'col')), parts along dimension 1
- normal_residual: float32 [64, 4096], P(None, ('rig', 'col')), parts along dimension 1
There are 2 independent parts, one for each index of `rig`. A program takes and returns all parts, laid end to end along the dimension named above; each array names one. Nothing has to cross between parts.
Inputs may be any that keep to these rules, and one draw needn't show every extreme that they name: `counts`: live slots of one cell; 1024 is reached on some cell and 128 on another in every draw.
All inputs are finite; a program needn't handle non-finite values.
Results may differ from a plain program's by a relative error of at most 0.0003.
Values sent between devices are 32-bit elements; how exact they have to be, the bound alone decides.
A program may use at most 64 MiB of HBM per device.

v0:
```python
import jax
import jax.numpy as jnp
from jax import lax
from jax.sharding import PartitionSpec as P

ITERS = 2


def slot_terms(blocks, gathered, transposed):
    if transposed:
        return jnp.sum(blocks * gathered[:, None, :], axis=0)
    return jnp.sum(blocks * gathered[None, :, :], axis=1)


def spread(terms, index, width):
    onehot = (index[:, None] == jnp.arange(width, dtype=jnp.int32)[None, :]).astype(jnp.float32)
    return jnp.dot(terms, onehot, precision=lax.Precision.HIGHEST)


def block_product(blocks, src_index, dst_index, count, source, width, transposed):
    slots_all = src_index.shape[0]
    live = (jnp.arange(slots_all, dtype=jnp.int32) < count).astype(jnp.float32)
    gathered = jnp.take(source, src_index, axis=1)
    terms = slot_terms(blocks, gathered, transposed) * live
    return spread(terms, dst_index, width)


def pull_back(blocks, rows_idx, cols_idx, count, source, width):
    partial_sum = block_product(blocks, rows_idx, cols_idx, count, source, width, True)
    return lax.psum(partial_sum, "row")


def param_total(value):
    return lax.psum(value, "col")


def curvature(image_part, damped_part):
    return lax.psum(image_part, "row") + param_total(damped_part)


def finish(step_field, normal_residual):
    return (step_field, normal_residual)


def on_device(jacobian, block_rows, block_cols, counts, residuals, damping):
    blocks = jacobian[0, 0]
    rows_idx = block_rows[0, 0]
    cols_idx = block_cols[0, 0]
    count = counts[0, 0]
    res_width = residuals.shape[1]
    par_width = damping.shape[1]
    rhs = -pull_back(blocks, rows_idx, cols_idx, count, residuals, par_width)
    step_field = jnp.zeros_like(rhs)
    normal_residual = rhs
    direction = rhs
    norm_now = param_total(jnp.sum(normal_residual * normal_residual))
    for step in range(ITERS):
        full_direction = direction
        image_part = block_product(
            blocks, cols_idx, rows_idx, count, full_direction, res_width, False
        )
        image = lax.psum(image_part, "col")
        damped_part = jnp.sum(direction * damping * direction)
        curv = curvature(jnp.sum(image * image), damped_part)
        alpha = norm_now / curv
        step_field = step_field + alpha * direction
        pulled = (
            pull_back(blocks, rows_idx, cols_idx, count, image, par_width) + damping * direction
        )
        normal_residual = normal_residual - alpha * pulled
        norm_next = param_total(jnp.sum(normal_residual * normal_residual))
        direction = normal_residual + norm_next / norm_now * direction
        norm_now = norm_next
    return finish(step_field, normal_residual)


def solution(mesh):
    placed = (
        P(("rig", "row"), "col", None, None, None),
        P(("rig", "row"), "col", None),
        P(("rig", "row"), "col", None),
        P(("rig", "row"), "col"),
        P(None, ("rig", "row")),
        P(None, ("rig", "col")),
    )
    return jax.shard_map(
        on_device,
        mesh=mesh,
        in_specs=placed,
        out_specs=(P(None, ("rig", "col")), P(None, ("rig", "col"))),
        check_vma=False,
    )
```

profile of v0, /device:TPU:0, one launch (start us, length us, event | category | flops | bytes accessed | tf_op | source)
XLA Modules:
  0.0 255.2 jit_solution(3975279527948880442)
XLA Ops:
  7.2 0.0 copy-start.5
  7.2 0.0 copy-start
  7.2 0.0 all-reduce.7.cloned.1.call-start
  7.2 0.7 compare_and_fusion.1
  8.0 0.7 fusion.26
  9.3 1.0 copy.8
  10.3 2.8 %gather_fusion = f32[1024,64]{1,0:T(8,128)S(1)} fusion(f32[64,512]{0,1:T(8,128)S(1)} %copy.8, s32[1024]{0:T(1024)S(1)} %fusion.26), kind=kCustom, calls=%fused_computation.clone | custom fusion | bytes 528384 | tf_op jit(solution)/shard_map/jit(_take)/gather | solution.py:23
  13.2 0.2 select_bitcast_fusion.4
  13.4 0.2 copy.9
  13.6 5.7 %fusion = f32[64,1024]{1,0:T(8,128)S(1)} fusion(bf16[1,1,64,64,1024]{4,3,2,1,0:T(8,128)(2,1)} %param.8, f32[64,1024]{1,0:T(8,128)S(1)} %copy.9), kind=kLoop, calls=%fused_computation.10 | loop fusion | flops 12517376 | bytes 8912896 | tf_op jit(solution)/shard_map/reduce_sum | solution.py:11
  19.2 0.0 copy-done.5
  19.2 1.6 fusion.9
  20.9 0.0 all-reduce.7.cloned.1.call-update
  20.9 0.0 all-reduce.9.cloned.1.call-start
  21.0 37.2 %all-reduce.7.cloned.1.call-done = f32[64,512]{1,0:T(8,128)} async-done(((f32[64,512]{1,0:T(8,128)}), f32[64,512]{1,0:T(8,128)}) %all-reduce.7.cloned.1.call-update) | async-done | bytes 131088 | tf_op jit(solution)/shard_map/psum | solution.py:30
  58.2 0.0 copy-done
  58.2 1.6 multiply_reduce_fusion.3
  59.8 0.1 copy.10
  59.9 2.8 %gather_fusion.1 = f32[1024,64]{1,0:T(8,128)S(1)} fusion(f32[64,512]{0,1:T(8,128)S(1)} %copy.10, s32[1024]{0:T(1024)S(1)} %fusion.27), kind=kCustom, calls=%fused_computation.1.clone | custom fusion | bytes 528384 | tf_op jit(solution)/shard_map/jit(_take)/gather | solution.py:23
  62.8 0.2 select_bitcast_fusion.3
  63.0 0.2 copy.11
  63.2 6.2 %fusion.1 = f32[64,1024]{1,0:T(8,128)S(1)} fusion(bf16[1,1,64,64,1024]{4,3,2,1,0:T(8,128)(2,1)} %param.8, f32[64,1024]{1,0:T(8,128)S(1)} %copy.11), kind=kLoop, calls=%fused_computation.11 | loop fusion | flops 12517376 | bytes 8912896 | tf_op jit(solution)/shard_map/reduce_sum | solution.py:12
  69.3 0.0 copy-done.4
  69.3 1.6 fusion.6
  70.9 0.0 all-reduce.9.cloned.1.call-update
  71.0 0.0 all-reduce.11.cloned.1.call-start
  71.0 31.1 %all-reduce.9.cloned.1.call-done = f32[64,512]{1,0:T(8,128)} async-done(((f32[64,512]{1,0:T(8,128)}), f32[64,512]{1,0:T(8,128)}) %all-reduce.9.cloned.1.call-update) | async-done | bytes 131088 | tf_op jit(solution)/shard_map/psum | solution.py:62
  102.2 1.1 copy.12
  103.3 2.8 %gather_fusion.2 = f32[1024,64]{1,0:T(8,128)S(1)} fusion(f32[64,512]{0,1:T(8,128)S(1)} %copy.12, s32[1024]{0:T(1024)S(1)} %fusion.26), kind=kCustom, calls=%fused_computation.2.clone | custom fusion | bytes 528384 | tf_op jit(solution)/shard_map/jit(_take)/gather | solution.py:23
  106.1 0.2 select_bitcast_fusion.2
  106.3 0.2 copy.13
  106.5 5.7 %fusion.2 = f32[64,1024]{1,0:T(8,128)S(1)} fusion(bf16[1,1,64,64,1024]{4,3,2,1,0:T(8,128)(2,1)} %param.8, f32[64,1024]{1,0:T(8,128)S(1)} %copy.13), kind=kLoop, calls=%fused_computation.12 | loop fusion | flops 12517376 | bytes 8912896 | tf_op jit(solution)/shard_map/reduce_sum | solution.py:11
  112.1 1.6 fusion.8
  113.7 0.0 all-reduce.11.cloned.1.call-update
  113.8 0.0 all-reduce.13.cloned.1.call-start
  113.8 0.0 copy-done.3
  113.8 0.7 multiply_reduce_fusion.4
  114.5 6.4 %all-reduce = (f32[]{:T(128)}, f32[]{:T(128)}) all-reduce(f32[]{:T(128)} %get-tuple-element.4, f32[]{:T(128)} %get-tuple-element.3), channel_id=1, replica_groups=mesh['rig'=2,'row'=4,'col'=4] {'col'}, use_global_device_ids=true, to_apply=%region_3.5 | all-reduce | flops 2 | bytes 16 | tf_op jit(solution)/shard_map/psum | solution.py:34
  120.9 12.6 %psum.80 = f32[]{:T(128)} all-reduce(f32[]{:T(128)} %multiply_reduce_fusion.4), channel_id=1, replica_groups=mesh['rig'=2,'row'=4,'col'=4] {'row'}, use_global_device_ids=true, to_apply=%region_7.9 | all-reduce | flops 1 | bytes 8 | tf_op jit(solution)/shard_map/psum | solution.py:38
  135.4 12.9 %all-reduce.11.cloned.1.call-done = f32[64,512]{1,0:T(8,128)} async-done(((f32[64,512]{1,0:T(8,128)}), f32[64,512]{1,0:T(8,128)}) %all-reduce.11.cloned.1.call-update) | async-done | bytes 131088 | tf_op jit(solution)/shard_map/psum | solution.py:30
  148.4 1.5 multiply_reduce_fusion.2
  149.9 6.3 %psum.83 = f32[]{:T(128)} all-reduce(f32[]{:T(128)} %get-tuple-element.9), channel_id=1, replica_groups=mesh['rig'=2,'row'=4,'col'=4] {'col'}, use_global_device_ids=true, to_apply=%region_13.15 | all-reduce | flops 1 | bytes 8 | tf_op jit(solution)/shard_map/psum | solution.py:34
  157.5 0.7 multiply_reduce_fusion
  158.2 0.1 copy.14
  158.3 2.8 %gather_fusion.3 = f32[1024,64]{1,0:T(8,128)S(1)} fusion(f32[64,512]{0,1:T(8,128)S(1)} %copy.14, s32[1024]{0:T(1024)S(1)} %fusion.27), kind=kCustom, calls=%fused_computation.3.clone | custom fusion | bytes 528384 | tf_op jit(solution)/shard_map/jit(_take)/gather | solution.py:23
  161.1 0.2 select_bitcast_fusion.1
  161.4 0.2 copy.15
  161.5 6.1 %fusion.3 = f32[64,1024]{1,0:T(8,128)S(1)} fusion(bf16[1,1,64,64,1024]{4,3,2,1,0:T(8,128)(2,1)} %param.8, f32[64,1024]{1,0:T(8,128)S(1)} %copy.15), kind=kLoop, calls=%fused_computation.13 | loop fusion | flops 12517376 | bytes 8912896 | tf_op jit(solution)/shard_map/reduce_sum | solution.py:12
  167.7 1.6 fusion.5
  169.3 0.0 all-reduce.13.cloned.1.call-update
  169.3 0.0 all-reduce.15.cloned.1.call-start
  169.4 31.4 %all-reduce.13.cloned.1.call-done = f32[64,512]{1,0:T(8,128)} async-done(((f32[64,512]{1,0:T(8,128)}), f32[64,512]{1,0:T(8,128)}) %all-reduce.13.cloned.1.call-update) | async-done | bytes 131088 | tf_op jit(solution)/shard_map/psum | solution.py:62
  200.8 1.1 copy.16
  201.9 2.8 %gather_fusion.4 = f32[1024,64]{1,0:T(8,128)S(1)} fusion(f32[64,512]{0,1:T(8,128)S(1)} %copy.16, s32[1024]{0:T(1024)S(1)} %fusion.26), kind=kCustom, calls=%fused_computation.4.clone | custom fusion | bytes 528384 | tf_op jit(solution)/shard_map/jit(_take)/gather | solution.py:23
  204.7 0.2 select_bitcast_fusion
  204.9 0.2 copy.17
  205.1 5.7 %fusion.4 = f32[64,1024]{1,0:T(8,128)S(1)} fusion(bf16[1,1,64,64,1024]{4,3,2,1,0:T(8,128)(2,1)} %param.8, f32[64,1024]{1,0:T(8,128)S(1)} %copy.17), kind=kLoop, calls=%fused_computation.14 | loop fusion | flops 12517376 | bytes 8912896 | tf_op jit(solution)/shard_map/reduce_sum | solution.py:11
  210.8 1.6 fusion.7
  212.4 0.0 all-reduce.15.cloned.1.call-update
  212.4 0.7 multiply_reduce_fusion.1
  213.1 6.4 %psum.86 = f32[]{:T(128)} all-reduce(f32[]{:T(128)} %get-tuple-element.7), channel_id=1, replica_groups=mesh['rig'=2,'row'=4,'col'=4] {'col'}, use_global_device_ids=true, to_apply=%region_19.21 | all-reduce | flops 1 | bytes 8 | tf_op jit(solution)/shard_map/psum | solution.py:34
  219.5 12.5 %psum.85 = f32[]{:T(128)} all-reduce(f32[]{:T(128)} %multiply_reduce_fusion.1), channel_id=1, replica_groups=mesh['rig'=2,'row'=4,'col'=4] {'row'}, use_global_device_ids=true, to_apply=%region_17.19 | all-reduce | flops 1 | bytes 8 | tf_op jit(solution)/shard_map/psum | solution.py:38
  233.8 13.2 %all-reduce.15.cloned.1.call-done = f32[64,512]{1,0:T(8,128)} async-done(((f32[64,512]{1,0:T(8,128)}), f32[64,512]{1,0:T(8,128)}) %all-reduce.15.cloned.1.call-update) | async-done | bytes 131088 | tf_op jit(solution)/shard_map/psum | solution.py:30
  247.0 1.7 multiply_subtract_fusion
  (9 shorter events, 0.0 us)
Async XLA Ops:
  7.2 12.1 %copy-start.5 = (s32[1,1,1024]{2,1,0:T(1,128)S(1)}, s32[1,1,1024]{2,1,0:T(1,128)}, u32[]{:S(2)}) copy-start(s32[1,1,1024]{2,1,0:T(1,128)} %param.10) | copy-start | bytes 12292
  7.2 51.0 %copy-start = (f32[64,512]{1,0:T(8,128)S(1)}, f32[64,512]{1,0:T(8,128)}, u32[]{:S(2)}) copy-start(f32[64,512]{1,0:T(8,128)} %param.13) | copy-start | bytes 393220
  7.2 51.0 %all-reduce.7.cloned.1.call-start = ((), (), s32[]{:S(2)}) async-start(), calls=%async_computation | async-start | bytes 262144 | tf_op jit(solution)/shard_map/psum | solution.py:30
  19.2 50.1 %copy-start.4 = (s32[1,1,1024]{2,1,0:T(1,128)S(1)}, s32[1,1,1024]{2,1,0:T(1,128)}, u32[]{:S(2)}) copy-start(s32[1,1,1024]{2,1,0:T(1,128)} %param.9) | copy-start | bytes 12292
  20.9 81.3 %all-reduce.9.cloned.1.call-start = ((), (), s32[]{:S(2)}) async-start(), calls=%async_computation.1 | async-start | bytes 262144 | tf_op jit(solution)/shard_map/psum | solution.py:62
  69.3 79.0 %copy-start.1 = (f32[64,512]{1,0:T(8,128)S(1)}, f32[64,512]{1,0:T(8,128)}, u32[]{:S(2)}) copy-start(f32[64,512]{1,0:T(8,128)} %all-reduce.7.cloned.1.call-done) | copy-start | bytes 393220
  71.0 77.4 %all-reduce.11.cloned.1.call-start = ((), (), s32[]{:S(2)}) async-start(), calls=%async_computation.2 | async-start | bytes 262144 | tf_op jit(solution)/shard_map/psum | solution.py:30
  102.2 11.7 %copy-start.3 = (f32[64,512]{1,0:T(8,128)S(1)}, f32[64,512]{1,0:T(8,128)}, u32[]{:S(2)}) copy-start(f32[64,512]{1,0:T(8,128)} %all-reduce.9.cloned.1.call-done) | copy-start | bytes 393220
  113.8 87.0 %all-reduce.13.cloned.1.call-start = ((), (), s32[]{:S(2)}) async-start(), calls=%async_computation.3 | async-start | bytes 262144 | tf_op jit(solution)/shard_map/psum | solution.py:62
  169.3 77.7 %all-reduce.15.cloned.1.call-start = ((), (), s32[]{:S(2)}) async-start(), calls=%async_computation.4 | async-start | bytes 262144 | tf_op jit(solution)/shard_map/psum | solution.py:30
  200.8 11.6 %copy-start.2 = (f32[64,512]{1,0:T(8,128)S(1)}, f32[64,512]{1,0:T(8,128)}, u32[]{:S(2)}) copy-start(f32[64,512]{1,0:T(8,128)} %all-reduce.13.cloned.1.call-done) | copy-start | bytes 393220
Sparse Core Ops, SparseCore 0:
  21.0 37.1 all-reduce.6
  71.1 31.0 all-reduce.8
  113.9 34.4 all-reduce.10
  169.4 31.2 all-reduce.12
  212.5 34.4 all-reduce.14
where the time goes:
time: 256 us; the launch traced here: 255 us
  waiting for transfers between devices  126 us (49%)
  blocking collectives  44.2 us (17%)
  other arithmetic  38.6 us (15%)
  between operations  19.8 us (8%)
  local copies, waits for them, and re-layouts  18.4 us (7%)
  matrix products  8.05 us (3%)
    psum x3, waiting for transfers between devices, pull_back(): return lax.psum(partial_sum, 'row')  63.3 us
    psum x2, waiting for transfers between devices, on_device(): image = lax.psum(image_part, 'col')  62.5 us
    psum x2, blocking collectives, curvature(): return lax.psum(image_part, 'row') + param_total(damped_part)  25.1 us
    psum x3, blocking collectives, param_total(): return lax.psum(value, 'col')  19 us
    reduce_sum x3, other arithmetic, slot_terms(): return jnp.sum(blocks * gathered[:, None, :], axis=0)  17 us
    gather x5, local copies, waits for them, and re-layouts, block_product(): gathered = jnp.take(source, src_index, axis=1)  14.1 us
    reduce_sum x2, other arithmetic, slot_terms(): return jnp.sum(blocks * gathered[None, :, :], axis=1)  12.3 us
    dot_general x5, matrix products, spread(): return jnp.dot(terms, onehot, precision=lax.Precision.HIGHEST)  8.05 us
  transfers between devices with their start and end apart: 5, of which 5 were waited for; matrix products, arithmetic and copies ran while one was open for 1% of the time, Pallas kernels for 0%

commit v1 on v0

v1 whole, which is shorter than its diff:
```python
import functools

import jax
import jax.numpy as jnp
from jax import lax
from jax.experimental import pallas as pl
from jax.experimental.pallas import tpu as pltpu
from jax.sharding import PartitionSpec as P

F32 = jnp.float32
BF16 = jnp.bfloat16
MESH = pl.DeviceIdType.MESH
LANES = 128
SUB = 8
LOADS = 4


class Group:
    def __init__(self, axis, size, rows):
        self.axis = axis
        self.n = size
        self.owners = min(size, 4)
        self.step = size // self.owners
        self.rows = rows // self.owners

    def locate(self):
        self.me = lax.axis_index(self.axis)
        self.mine = self.me // self.step

    def chunk(self, d):
        if d == 0:
            return self.mine
        if self.owners == 4:
            if d == 1:
                return self.mine + 1 - 2 * lax.rem(self.mine, 2)
            if d == 2:
                return lax.rem(self.mine + 2, 4)
            return 3 - self.mine
        return lax.rem(self.mine + d, self.owners)

    def peer(self, d):
        if self.n == self.owners:
            return self.chunk(d)
        return lax.rem(self.me + d, self.n)

    def when_owner(self, action):
        if self.step == 1:
            action()
        else:
            pl.when(lax.rem(self.me, self.step) == 0)(action)

    def when_not_owner(self, action):
        if self.step > 1:
            pl.when(lax.rem(self.me, self.step) != 0)(action)


class Sum:
    def __init__(self, group, k, part, recv, full, sems):
        self.g, self.k = group, k
        self.part, self.recv, self.full = part, recv, full
        self.rs_send, self.rs_recv, self.ag_send, self.ag_recv = sems

    def rs(self, c, src, target):
        return pltpu.make_async_remote_copy(
            src_ref=self.part.at[self.k, c],
            dst_ref=self.recv.at[self.k, src],
            send_sem=self.rs_send.at[self.k, c],
            recv_sem=self.rs_recv.at[self.k, src],
            device_id={self.g.axis: target},
            device_id_type=MESH,
        )

    def ag(self, c, target):
        return pltpu.make_async_remote_copy(
            src_ref=self.full.at[self.k, c],
            dst_ref=self.full.at[self.k, c],
            send_sem=self.ag_send.at[self.k, target],
            recv_sem=self.ag_recv.at[self.k, c],
            device_id={self.g.axis: target},
            device_id_type=MESH,
        )

    def scatter(self):
        g = self.g
        for d in reversed(range(g.owners)):
            c = g.chunk(d)
            if d == 0:
                g.when_not_owner(lambda: self.rs(g.mine, g.me, g.mine * g.step).start())
            else:
                self.rs(c, g.me, c * g.step).start()

    def reduce(self):
        g = self.g

        def own():
            total = self.part[self.k, g.mine]
            for d in range(1, g.n):
                src = g.peer(d)
                self.rs(g.mine, src, g.me).wait_recv()
                total = total + self.recv[self.k, src]
            self.full[self.k, g.mine] = total
            for d in reversed(range(1, g.n)):
                self.ag(g.mine, g.peer(d)).start()

        g.when_owner(own)

    def arrive(self, d):
        g = self.g
        c = g.chunk(d)
        if d == 0:
            g.when_not_owner(lambda: self.ag(c, g.me).wait_recv())
        else:
            self.ag(c, g.me).wait_recv()
        return c

    def drain(self):
        g = self.g
        for d in range(g.owners):
            c = g.chunk(d)
            if d == 0:
                g.when_not_owner(lambda: self.rs(g.mine, g.me, g.mine * g.step).wait_send())
            else:
                self.rs(c, g.me, c * g.step).wait_send()

        def own():
            for d in range(1, g.n):
                self.ag(g.mine, g.peer(d)).wait_send()

        g.when_owner(own)


class Tile:
    def __init__(self, group, k, buf, send, recv):
        self.g, self.k, self.buf, self.send, self.recv = group, k, buf, send, recv

    def copy(self, slot, target):
        return pltpu.make_async_remote_copy(
            src_ref=self.buf.at[self.k, slot],
            dst_ref=self.buf.at[self.k, slot],
            send_sem=self.send.at[self.k, target],
            recv_sem=self.recv.at[self.k, slot],
            device_id={self.g.axis: target},
            device_id_type=MESH,
        )

    def start(self, value):
        g = self.g
        self.buf[self.k, g.me] = value
        for d in range(1, g.n):
            self.copy(g.me, g.peer(d)).start()

    def total(self):
        g = self.g
        for d in range(1, g.n):
            self.copy(g.peer(d), g.me).wait_recv()
        total = self.buf[self.k, 0]
        for slot in range(1, g.n):
            total = total + self.buf[self.k, slot]
        return total

    def drain(self):
        for d in range(1, self.g.n):
            self.copy(self.g.me, self.g.peer(d)).wait_send()


def pieces(x):
    high = x.astype(BF16)
    low = (x - high.astype(F32)).astype(BF16)
    return jnp.concatenate([high, low], axis=0)


def fold(x):
    total = None
    for r in range(0, x.shape[0], SUB):
        for c in range(0, x.shape[1], LANES):
            block = x[r : r + SUB, c : c + LANES]
            total = block if total is None else total + block
    return total


def whole(tile):
    return jnp.sum(tile, axis=(0, 1), keepdims=True)


def kernel(
    row, col, jac_hbm, rows_ref, cols_ref, count_ref, res_ref, damp_ref, step_ref, out_ref,
    jac, oh_r, oh_c, g_ref, terms, acc3, r1_ref,
    part_r, recv_r, full_r, part_c, recv_c, full_c, tiles,
    load_sem, rs_send, rs_recv, ag_send, ag_recv, t_send, t_recv,
):
    entries, _, slots = jac.shape
    row.locate()
    col.locate()
    sems_r = (rs_send.at[0], rs_recv.at[0], ag_send.at[0], ag_recv.at[0])
    sems_c = (rs_send.at[1], rs_recv.at[1], ag_send.at[1], ag_recv.at[1])

    per = entries // LOADS

    def load(q):
        part = pl.ds(q * per, per)
        return pltpu.make_async_copy(jac_hbm.at[part], jac.at[part], load_sem.at[q])

    for q in range(LOADS):
        load(q).start()

    barrier = pltpu.get_barrier_semaphore()
    for g in (row, col):
        for d in range(1, g.n):
            pl.semaphore_signal(
                barrier, inc=1, device_id={g.axis: g.peer(d)}, device_id_type=MESH
            )

    live = lax.broadcasted_iota(jnp.int32, (1, slots), 1) < count_ref[0, 0]
    for idx_ref, oh in ((rows_ref, oh_r), (cols_ref, oh_c)):
        width = oh.shape[0]
        index = jnp.where(live, idx_ref[...], -1)
        step = 64

        def build(i, _, index=index, oh=oh, step=step):
            at = pl.multiple_of(i * step, step)
            ids = lax.broadcasted_iota(jnp.int32, (step, slots), 0) + at
            oh[pl.ds(at, step), :] = jnp.where(ids == index, 1.0, 0.0).astype(BF16)
            return 0

        lax.fori_loop(0, width // step, build, 0)

    def gather(x, oh):
        rows = x.shape[0]
        y = jnp.dot(pieces(x), oh[...], preferred_element_type=F32)
        g_ref[pl.ds(0, rows), :] = y[:rows] + y[rows:]

    def add_back(a0, rows, first):
        def body(kk, _):
            sl = pl.ds(pl.multiple_of(kk * LANES, LANES), LANES)
            acc = None if first else terms[:, sl]
            for a in range(rows):
                term = jac[a0 + a, :, sl].astype(F32) * g_ref[a : a + 1, sl]
                acc = term if acc is None else acc + term
            terms[:, sl] = acc
            return 0

        lax.fori_loop(0, slots // LANES, body, 0)

    def add_forth(b0, rows, first):
        b0 = pl.multiple_of(b0, rows)

        def body(kk, _):
            sl = pl.ds(pl.multiple_of(kk * LANES, LANES), LANES)
            g = g_ref[pl.ds(0, rows), sl]
            for a in range(entries):
                m = jac[a, pl.ds(b0, rows), sl].astype(F32) * g
                part = m[:SUB]
                for r in range(SUB, rows, SUB):
                    part = part + m[r : r + SUB]
                acc3[a, :, sl] = part if first else acc3[a, :, sl] + part
            return 0

        lax.fori_loop(0, slots // LANES, body, 0)

    def close_forth():
        def body(kk, _):
            sl = pl.ds(pl.multiple_of(kk * LANES, LANES), LANES)
            terms[:, sl] = jnp.sum(acc3[:, :, sl], axis=1)
            return 0

        lax.fori_loop(0, slots // LANES, body, 0)

    def spread(oh, s):
        y = lax.dot_general(
            pieces(terms[...]), oh[...], (((1,), (1,)), ((), ())), preferred_element_type=F32
        )
        out = y[:entries] + y[entries:]
        n = s.g.rows
        for c in range(s.g.owners):
            s.part[s.k, c] = out[c * n : (c + 1) * n]
        s.scatter()
        s.reduce()

    def sum_r(k):
        return Sum(row, k, part_r, recv_r, full_r, sems_r)

    def sum_c(k):
        return Sum(col, k, part_c, recv_c, full_c, sems_c)

    sums = [sum_r(0), sum_c(0), sum_r(1), sum_c(1), sum_r(2)]
    groups = (col, row, col, row, col)
    exchanges = [Tile(g, k, tiles, t_send, t_recv) for k, g in enumerate(groups)]
    nothing = jnp.zeros((SUB, LANES), F32)

    def pair(first, second=nothing):
        return jnp.concatenate([first, second], axis=0)

    def damp(c):
        return damp_ref[pl.ds(pl.multiple_of(c * row.rows, SUB), row.rows), :]

    def fold_all(group, value):
        total = value(0)
        for c in range(1, group.owners):
            total = total + value(c)
        return total

    for q in range(LOADS):
        gather(-res_ref[pl.ds(q * per, per), :], oh_r)
        load(q).wait()
        add_back(q * per, per, q == 0)
    pl.semaphore_wait(barrier, row.n + col.n - 2)
    spread(oh_c, sums[0])

    def p0(c):
        return full_r[0, c]

    for d in range(row.owners):
        c = sums[0].arrive(d)
        gather(p0(c), oh_c)
        if d == row.owners - 1:
            exchanges[0].start(pair(
                fold_all(row, lambda e: fold(p0(e) * p0(e))),
                fold_all(row, lambda e: fold(p0(e) * damp(e) * p0(e))),
            ))
        add_forth(c * row.rows, row.rows, d == 0)
    close_forth()
    spread(oh_r, sums[1])

    for d in range(col.owners):
        c = sums[1].arrive(d)
        gather(full_c[0, c], oh_r)
        if d == col.owners - 1:
            exchanges[1].start(pair(fold_all(col, lambda e: fold(full_c[0, e] * full_c[0, e]))))
        add_back(c * col.rows, col.rows, d == 0)
    spread(oh_c, sums[2])

    both = exchanges[0].total()
    norm0 = whole(both[:SUB])
    alpha0 = norm0 / (whole(exchanges[1].total()[:SUB]) + whole(both[SUB:]))

    for d in range(row.owners):
        c = sums[2].arrive(d)
        r1 = p0(c) - alpha0 * (full_r[1, c] + damp(c) * p0(c))
        r1_ref[c] = r1
        gather(r1, oh_c)
        if d == row.owners - 1:
            exchanges[2].start(pair(fold_all(row, lambda e: fold(r1_ref[e] * r1_ref[e]))))
        add_forth(c * row.rows, row.rows, d == 0)
    close_forth()
    spread(oh_r, sums[3])

    norm1 = whole(exchanges[2].total()[:SUB])
    beta = norm1 / norm0

    def p1(c):
        return r1_ref[c] + beta * p0(c)

    def image1(c):
        return full_c[1, c] + beta * full_c[0, c]

    exchanges[4].start(pair(fold_all(row, lambda e: fold(p1(e) * damp(e) * p1(e)))))
    for d in range(col.owners):
        c = sums[3].arrive(d)
        gather(image1(c), oh_r)
        if d == col.owners - 1:
            exchanges[3].start(pair(fold_all(col, lambda e: fold(image1(e) * image1(e)))))
        add_back(c * col.rows, col.rows, d == 0)
    spread(oh_c, sums[4])

    curv1 = whole(exchanges[3].total()[:SUB]) + whole(exchanges[4].total()[:SUB])
    alpha1 = norm1 / curv1
    for d in range(row.owners):
        c = sums[4].arrive(d)
        at = pl.ds(pl.multiple_of(c * row.rows, SUB), row.rows)
        step_ref[at, :] = alpha0 * p0(c) + alpha1 * p1(c)
        out_ref[at, :] = r1_ref[c] - alpha1 * (full_r[2, c] + damp(c) * p1(c))

    for s in sums:
        s.drain()
    for e in exchanges:
        e.drain()


def on_device(n_row, n_col, jacobian, block_rows, block_cols, counts, residuals, damping):
    entries, _, slots = jacobian.shape[2:]
    res_width = residuals.shape[1]
    par_width = damping.shape[1]
    row = Group("row", n_row, entries)
    col = Group("col", n_col, entries)
    n = max(n_row, n_col)
    own = max(row.owners, col.owners)
    vmem = pl.BlockSpec(memory_space=pltpu.VMEM)
    dma = pltpu.SemaphoreType.DMA
    out = jax.ShapeDtypeStruct((entries, par_width), F32)
    return pl.pallas_call(
        functools.partial(kernel, row, col),
        out_shape=(out, out),
        in_specs=[
            pl.BlockSpec(memory_space=pl.ANY),
            vmem,
            vmem,
            pl.BlockSpec(memory_space=pltpu.SMEM),
            vmem,
            vmem,
        ],
        out_specs=(vmem, vmem),
        scratch_shapes=[
            pltpu.VMEM((entries, entries, slots), BF16),
            pltpu.VMEM((res_width, slots), BF16),
            pltpu.VMEM((par_width, slots), BF16),
            pltpu.VMEM((max(row.rows, col.rows), slots), F32),
            pltpu.VMEM((entries, slots), F32),
            pltpu.VMEM((entries, SUB, slots), F32),
            pltpu.VMEM((row.owners, row.rows, par_width), F32),
            pltpu.VMEM((3, row.owners, row.rows, par_width), F32),
            pltpu.VMEM((3, n_row, row.rows, par_width), F32),
            pltpu.VMEM((3, row.owners, row.rows, par_width), F32),
            pltpu.VMEM((2, col.owners, col.rows, res_width), F32),
            pltpu.VMEM((2, n_col, col.rows, res_width), F32),
            pltpu.VMEM((2, col.owners, col.rows, res_width), F32),
            pltpu.VMEM((5, n, 2 * SUB, LANES), F32),
            dma((LOADS,)),
            dma((2, 3, own)),
            dma((2, 3, n)),
            dma((2, 3, n)),
            dma((2, 3, own)),
            dma((5, n)),
            dma((5, n)),
        ],
        compiler_params=pltpu.CompilerParams(
            collective_id=0, has_side_effects=True, vmem_limit_bytes=48 * 1024 * 1024
        ),
        cost_estimate=pl.CostEstimate(
            flops=10 * entries * entries * slots,
            bytes_accessed=2 * entries * entries * slots,
            transcendentals=0,
        ),
        name="cg",
    )(
        jacobian.reshape(entries, entries, slots),
        block_rows.reshape(1, slots),
        block_cols.reshape(1, slots),
        counts,
        residuals,
        damping,
    )


def solution(mesh):
    placed = (
        P(("rig", "row"), "col", None, None, None),
        P(("rig", "row"), "col", None),
        P(("rig", "row"), "col", None),
        P(("rig", "row"), "col"),
        P(None, ("rig", "row")),
        P(None, ("rig", "col")),
    )
    return jax.shard_map(
        functools.partial(on_device, mesh.shape["row"], mesh.shape["col"]),
        mesh=mesh,
        in_specs=placed,
        out_specs=(P(None, ("rig", "col")), P(None, ("rig", "col"))),
        check_vma=False,
    )
```

time: 256 us -> 67 us (0.26)
  waiting for transfers between devices: 126 us -> 0 us
  Pallas kernels: 0 us -> 61 us
  blocking collectives: 44.2 us -> 0 us
  other arithmetic: 38.6 us -> 0 us
  between operations: 19.8 us -> 1.3 us
  local copies, waits for them, and re-layouts: 18.4 us -> 4.49 us
  matrix products: 8.05 us -> 0 us
    psum x5 -> x0, waiting for transfers between devices: 126 us -> none  [the longest x3 63.3 us: pull_back(): return lax.psum(partial_sum, 'row')]
    pallas_call x0 -> x1, Pallas kernels: none -> 61 us  [on_device(): pl.pallas_call(functools.partial(kernel, row, col), out_shape=(out, out),...]
    psum x5 -> x0, blocking collectives: 44.2 us -> none  [the longest x2 25.1 us: curvature(): return lax.psum(image_part, 'row') + param_total(damped_part)]
    reduce_sum x10 -> x0, other arithmetic: 34.5 us -> none  [the longest x3 17 us: slot_terms(): return jnp.sum(blocks * gathered[:, None, :], axis=0)]
    gather x5 -> x0, local copies, waits for them, and re-layouts: 14.1 us -> none  [block_product(): gathered = jnp.take(source, src_index, axis=1)]
    dot_general x5 -> x0, matrix products: 8.05 us -> none  [spread(): return jnp.dot(terms, onehot, precision=lax.Precision.HIGHEST)]
    unnamed x13 -> x10, local copies, waits for them, and re-layouts: 1.05 us -> 4.49 us
  transfers between devices with their start and end apart: 5 -> 0, of which waited for: 5 -> 0; matrix products, arithmetic and copies ran while one was open for 1% -> 0% of each run, Pallas kernels for 0% -> 0%
where the time goes in v1:
time: 67 us; the launch traced here: 66.8 us
  Pallas kernels  61 us (91%)
  local copies, waits for them, and re-layouts  4.49 us (7%)
  between operations  1.3 us (2%)
    pallas_call x1, Pallas kernels, on_device(): pl.pallas_call(functools.partial(kernel, row, col), out_shape=(out, out),...  61 us
    unnamed x10, local copies, waits for them, and re-layouts  4.49 us

profile of v1, /device:TPU:0, one launch (start us, length us, event | category | flops | bytes accessed | tf_op | source)
XLA Modules:
  0.0 66.8 jit_solution(4520852189840076916)
XLA Ops:
  1.3 0.0 copy-start
  1.3 0.9 %copy-done = f32[64,512]{1,0:T(8,128)S(1)} copy-done((f32[64,512]{1,0:T(8,128)S(1)}, f32[64,512]{1,0:T(8,128)}, u32[]{:S(2)}) %copy-start) | copy-done | bytes 131096
  2.2 0.0 copy-start.1
  2.2 0.9 %copy-done.1 = f32[64,512]{1,0:T(8,128)S(1)} copy-done((f32[64,512]{1,0:T(8,128)S(1)}, f32[64,512]{1,0:T(8,128)}, u32[]{:S(2)}) %copy-start.1) | copy-done | bytes 131096
  3.1 0.0 copy-start.2
  3.1 0.7 %copy-done.2 = s32[1,1,1024]{2,1,0:T(1,128)S(1)} copy-done((s32[1,1,1024]{2,1,0:T(1,128)S(1)}, s32[1,1,1024]{2,1,0:T(1,128)}, u32[]{:S(2)}) %copy-start.2) | copy-done | bytes 4120
  3.8 0.0 copy-start.3
  3.8 0.7 %copy-done.3 = s32[1,1,1024]{2,1,0:T(1,128)S(1)} copy-done((s32[1,1,1024]{2,1,0:T(1,128)S(1)}, s32[1,1,1024]{2,1,0:T(1,128)}, u32[]{:S(2)}) %copy-start.3) | copy-done | bytes 4120
  4.5 61.0 %cg.1 = (f32[64,512]{1,0:T(8,128)S(1)}, f32[64,512]{1,0:T(8,128)S(1)}) custom-call(bf16[64,64,1024]{2,1,0:T(8,128)(2,1)} %bitcast.5, s32[1,1024]{1,0:T(1,128)S(1)} %bitcast.3, s32[1,1024]{1,0:T(1,128)S(1)} %bitcast.4, s32[1,1]{1,0:T(1,128)S(6)} %copy.10.count_ref, f32[64,512]{1,0:T(8,128)S(1)} %copy-done, f32[64,512]{1,0:T(8,128)S(1)} %copy-done.1), custom_call_target="tpu_custom_call" | custom-call | flops 41943040 | bytes 8388608 | tf_op jit(solution)/shard_map/cg/pallas_call | solution.py:390
  65.5 0.7 copy.11
  66.1 0.7 copy.12
Async XLA Ops:
  1.3 0.9 %copy-start = (f32[64,512]{1,0:T(8,128)S(1)}, f32[64,512]{1,0:T(8,128)}, u32[]{:S(2)}) copy-start(f32[64,512]{1,0:T(8,128)} %res_ref.1) | copy-start | bytes 393220
  2.2 0.9 %copy-start.1 = (f32[64,512]{1,0:T(8,128)S(1)}, f32[64,512]{1,0:T(8,128)}, u32[]{:S(2)}) copy-start(f32[64,512]{1,0:T(8,128)} %damp_ref.1) | copy-start | bytes 393220
  3.1 0.7 %copy-start.2 = (s32[1,1,1024]{2,1,0:T(1,128)S(1)}, s32[1,1,1024]{2,1,0:T(1,128)}, u32[]{:S(2)}) copy-start(s32[1,1,1024]{2,1,0:T(1,128)} %param.7) | copy-start | bytes 12292
  3.8 0.7 %copy-start.3 = (s32[1,1,1024]{2,1,0:T(1,128)S(1)}, s32[1,1,1024]{2,1,0:T(1,128)}, u32[]{:S(2)}) copy-start(s32[1,1,1024]{2,1,0:T(1,128)} %param.8) | copy-start | bytes 12292

commit v2 on v1

v2 whole, which is shorter than its diff:
```python
import functools

import jax
import jax.numpy as jnp
from jax import lax
from jax.experimental import pallas as pl
from jax.experimental.pallas import tpu as pltpu
from jax.sharding import PartitionSpec as P

F32 = jnp.float32
BF16 = jnp.bfloat16
MESH = pl.DeviceIdType.MESH
LANES = 128
SUB = 8
LOADS = 4
HALVES = 2
PIECES = 2


class Group:
    def __init__(self, axis, size):
        self.axis, self.n = axis, size

    def locate(self):
        self.me = lax.axis_index(self.axis)

    def peer(self, d):
        return lax.rem(self.me + d, self.n)

    def remote(self, src, dst, send, recv, target):
        return pltpu.make_async_remote_copy(
            src_ref=src, dst_ref=dst, send_sem=send, recv_sem=recv,
            device_id={self.axis: target}, device_id_type=MESH,
        )


class LineSum:
    def __init__(self, group, k, part, recv, full, sems):
        self.g, self.k = group, k
        self.part, self.recv, self.full = part, recv, full
        self.rs_send, self.rs_recv, self.ag_send, self.ag_recv = sems
        self.base = group.n // 2 - 1
        self.near = jnp.where(group.me <= self.base, 0, 1)

    def piece(self, q):
        rows = self.part.shape[2] // PIECES
        return pl.ds(q * rows, rows)

    def rs(self, c, q, src, target):
        k, at = self.k, self.piece(q)
        return self.g.remote(
            self.part.at[k, c, at], self.recv.at[k, src, at],
            self.rs_send.at[k, c, q], self.rs_recv.at[k, src, q], target,
        )

    def ag(self, c, q, target):
        k, at = self.k, self.piece(q)
        return self.g.remote(
            self.full.at[k, c, at], self.full.at[k, c, at],
            self.ag_send.at[k, target, q], self.ag_recv.at[k, c, q], target,
        )

    def is_owner(self):
        return self.g.me == self.base + self.near

    def places(self):
        toward = 1 - 2 * self.near
        half = self.g.n // 2
        steps = list(range(half, 0, -1)) + [-e for e in range(half - 1, 0, -1)]
        return [self.g.me + toward * e for e in steps]

    def order(self):
        return (1 - self.near, self.near)

    def send(self, place):
        g, c = self.g, self.order()[place]

        def start():
            for q in range(PIECES):
                self.rs(c, q, g.me, self.base + c).start()

        if place == 0:
            start()
        else:
            pl.when(jnp.logical_not(self.is_owner()))(start)

    def reduce(self):
        @pl.when(self.is_owner())
        def _():
            for q in range(PIECES):
                at = self.piece(q)
                total = self.part[self.k, self.near, at, :]
                for src in reversed(self.places()):
                    self.rs(self.near, q, src, self.g.me).wait_recv()
                    total = total + self.recv[self.k, src, at, :]
                self.full[self.k, self.near, at, :] = total
                for target in self.places():
                    self.ag(self.near, q, target).start()

    def arrive(self, d):
        if d == 0:
            @pl.when(jnp.logical_not(self.is_owner()))
            def _():
                for q in range(PIECES):
                    self.ag(self.near, q, self.g.me).wait_recv()

            return self.near
        for q in range(PIECES):
            self.ag(1 - self.near, q, self.g.me).wait_recv()
        return 1 - self.near

    def drain(self):
        g, far = self.g, 1 - self.near
        for q in range(PIECES):
            self.rs(far, q, g.me, self.base + far).wait_send()

        @pl.when(jnp.logical_not(self.is_owner()))
        def _():
            for q in range(PIECES):
                self.rs(self.near, q, g.me, self.base + self.near).wait_send()

        @pl.when(self.is_owner())
        def _():
            for q in range(PIECES):
                for target in self.places():
                    self.ag(self.near, q, target).wait_send()


class PairSum:
    def __init__(self, group, k, part, recv, halves, full, sems):
        self.g, self.k = group, k
        self.part, self.recv, self.halves, self.full = part, recv, halves, full
        self.a_send, self.a_recv, self.x_send, self.x_recv, self.b_send, self.b_recv = sems
        self.h = lax.rem(group.me, 2)
        self.chip = group.me // 2
        self.chips = group.n // 2
        self.pair = group.me + 1 - 2 * self.h

    def first(self, c):
        k = self.k
        return self.g.remote(
            self.part.at[k, c], self.recv.at[k], self.a_send.at[k], self.a_recv.at[k], self.pair
        )

    def cross(self, slot, chip):
        k = self.k
        return self.g.remote(
            self.halves.at[k, slot], self.halves.at[k, slot],
            self.x_send.at[k, chip], self.x_recv.at[k, slot], 2 * chip + self.h,
        )

    def last(self, c):
        k = self.k
        return self.g.remote(
            self.full.at[k, c], self.full.at[k, c], self.b_send.at[k], self.b_recv.at[k], self.pair
        )

    def others(self):
        return [lax.rem(self.chip + e, self.chips) for e in range(1, self.chips)]

    def order(self):
        return (1 - self.h, self.h)

    def send(self, place):
        if place == 0:
            self.first(1 - self.h).start()

    def reduce(self):
        k = self.k
        self.first(self.h).wait_recv()
        self.halves[k, self.chip] = self.part[k, self.h] + self.recv[k]
        for chip in self.others():
            self.cross(self.chip, chip).start()
        for chip in self.others():
            self.cross(chip, chip).wait_recv()
        total = self.halves[k, 0]
        for slot in range(1, self.chips):
            total = total + self.halves[k, slot]
        self.full[k, self.h] = total
        self.last(self.h).start()

    def arrive(self, d):
        if d == 0:
            return self.h
        self.last(1 - self.h).wait_recv()
        return 1 - self.h

    def drain(self):
        self.first(1 - self.h).wait_send()
        for chip in self.others():
            self.cross(self.chip, chip).wait_send()
        self.last(self.h).wait_send()


class Tile:
    def __init__(self, group, k, buf, send, recv):
        self.g, self.k, self.buf, self.send, self.recv = group, k, buf, send, recv

    def copy(self, slot, target):
        return pltpu.make_async_remote_copy(
            src_ref=self.buf.at[self.k, slot],
            dst_ref=self.buf.at[self.k, slot],
            send_sem=self.send.at[self.k, target],
            recv_sem=self.recv.at[self.k, slot],
            device_id={self.g.axis: target},
            device_id_type=MESH,
        )

    def start(self, value):
        g = self.g
        self.buf[self.k, g.me] = value
        for d in range(1, g.n):
            self.copy(g.me, g.peer(d)).start()

    def total(self):
        g = self.g
        for d in range(1, g.n):
            self.copy(g.peer(d), g.me).wait_recv()
        total = self.buf[self.k, 0]
        for slot in range(1, g.n):
            total = total + self.buf[self.k, slot]
        return total

    def drain(self):
        for d in range(1, self.g.n):
            self.copy(self.g.me, self.g.peer(d)).wait_send()


def pieces(x):
    high = x.astype(BF16)
    low = (x - high.astype(F32)).astype(BF16)
    return jnp.concatenate([high, low], axis=0)


def fold(x):
    total = None
    for r in range(0, x.shape[0], SUB):
        for c in range(0, x.shape[1], LANES):
            block = x[r : r + SUB, c : c + LANES]
            total = block if total is None else total + block
    return total


def whole(tile):
    return jnp.sum(tile, axis=(0, 1), keepdims=True)


def kernel(
    row, col, jac_hbm, rows_hbm, cols_hbm, count_ref, res_hbm, damp_hbm, step_ref, out_ref,
    jac, rows_ref, cols_ref, res_ref, damp_ref, oh_r, oh_c, g_ref, terms, acc3, r1_ref,
    part_r, recv_r, full_r, part_c, recv_c, halves, full_c, tiles,
    load_sem, small_sem, rs_send, rs_recv, ag_send, ag_recv,
    a_send, a_recv, x_send, x_recv, b_send, b_recv, t_send, t_recv,
):
    entries, _, slots = jac.shape
    rows = entries // HALVES
    row.locate()
    col.locate()
    sems_r = (rs_send, rs_recv, ag_send, ag_recv)
    sems_c = (a_send, a_recv, x_send, x_recv, b_send, b_recv)

    barrier = pltpu.get_barrier_semaphore()
    for g in (row, col):
        for d in range(1, g.n):
            pl.semaphore_signal(
                barrier, inc=1, device_id={g.axis: g.peer(d)}, device_id_type=MESH
            )

    small = [
        pltpu.make_async_copy(src, dst, small_sem.at[q])
        for q, (src, dst) in enumerate((
            (rows_hbm, rows_ref), (cols_hbm, cols_ref), (res_hbm, res_ref), (damp_hbm, damp_ref),
        ))
    ]
    for copy in small:
        copy.start()
    per = entries // LOADS

    def load(q):
        part = pl.ds(q * per, per)
        return pltpu.make_async_copy(jac_hbm.at[part], jac.at[part], load_sem.at[q])

    for q in range(LOADS):
        load(q).start()
    for copy in small:
        copy.wait()

    live = lax.broadcasted_iota(jnp.int32, (1, slots), 1) < count_ref[0, 0]
    for idx_ref, oh in ((rows_ref, oh_r), (cols_ref, oh_c)):
        width = oh.shape[0]
        index = jnp.where(live, idx_ref[...], -1)
        step = 64

        def build(i, _, index=index, oh=oh, step=step):
            at = pl.multiple_of(i * step, step)
            ids = lax.broadcasted_iota(jnp.int32, (step, slots), 0) + at
            oh[pl.ds(at, step), :] = jnp.where(ids == index, 1.0, 0.0).astype(BF16)
            return 0

        lax.fori_loop(0, width // step, build, 0)

    def gather(x, oh):
        count = x.shape[0]
        y = jnp.dot(pieces(x), oh[...], preferred_element_type=F32)
        g_ref[pl.ds(0, count), :] = y[:count] + y[count:]

    def add_back(a0, count, first, half=None):
        width = entries if half is None else rows
        b0 = 0 if half is None else pl.multiple_of(half * rows, rows)

        def body(kk, _):
            sl = pl.ds(pl.multiple_of(kk * LANES, LANES), LANES)
            acc = None if first else terms[pl.ds(b0, width), sl]
            for a in range(count):
                term = jac[a0 + a, pl.ds(b0, width), sl].astype(F32) * g_ref[a : a + 1, sl]
                acc = term if acc is None else acc + term
            terms[pl.ds(b0, width), sl] = acc
            return 0

        lax.fori_loop(0, slots // LANES, body, 0)

    def add_forth(b0, count, first, half=None):
        width = entries if half is None else rows
        a0 = 0 if half is None else pl.multiple_of(half * rows, rows)
        b0 = pl.multiple_of(b0, count)

        def body(kk, _):
            sl = pl.ds(pl.multiple_of(kk * LANES, LANES), LANES)
            g = g_ref[pl.ds(0, count), sl]
            for a in range(width):
                m = jac[a0 + a, pl.ds(b0, count), sl].astype(F32) * g
                part = m[:SUB]
                for r in range(SUB, count, SUB):
                    part = part + m[r : r + SUB]
                acc3[a0 + a, :, sl] = part if first else acc3[a0 + a, :, sl] + part
            if half is not None:
                terms[pl.ds(a0, width), sl] = jnp.sum(acc3[pl.ds(a0, width), :, sl], axis=1)
            return 0

        lax.fori_loop(0, slots // LANES, body, 0)

    def finish(s, oh, work):
        for place, half in enumerate(s.order()):
            work(half)
            y = lax.dot_general(
                pieces(terms[pl.ds(pl.multiple_of(half * rows, rows), rows), :]), oh[...],
                (((1,), (1,)), ((), ())), preferred_element_type=F32,
            )
            s.part[s.k, half] = y[:rows] + y[rows:]
            s.send(place)
        s.reduce()

    def sum_r(k):
        return LineSum(row, k, part_r, recv_r, full_r, sems_r)

    def sum_c(k):
        return PairSum(col, k, part_c, recv_c, halves, full_c, sems_c)

    sums = [sum_r(0), sum_c(0), sum_r(1), sum_c(1), sum_r(2)]
    groups = (col, row, col, row, col)
    exchanges = [Tile(g, k, tiles, t_send, t_recv) for k, g in enumerate(groups)]
    nothing = jnp.zeros((SUB, LANES), F32)

    def pair(first, second=nothing):
        return jnp.concatenate([first, second], axis=0)

    def damp(c):
        return damp_ref[pl.ds(pl.multiple_of(c * rows, rows), rows), :]

    def fold_all(value):
        total = value(0)
        for c in range(1, HALVES):
            total = total + value(c)
        return total

    for q in range(LOADS):
        gather(-res_ref[pl.ds(q * per, per), :], oh_r)
        load(q).wait()
        if q < LOADS - 1:
            add_back(q * per, per, q == 0)
    pl.semaphore_wait(barrier, row.n + col.n - 2)
    finish(sums[0], oh_c, lambda half: add_back((LOADS - 1) * per, per, False, half))

    def p0(c):
        return full_r[0, c]

    for d in range(HALVES):
        c = sums[0].arrive(d)
        gather(p0(c), oh_c)
        if d == HALVES - 1:
            exchanges[0].start(pair(
                fold_all(lambda e: fold(p0(e) * p0(e))),
                fold_all(lambda e: fold(p0(e) * damp(e) * p0(e))),
            ))
        if d < HALVES - 1:
            add_forth(c * rows, rows, True)
    finish(sums[1], oh_r, lambda half: add_forth(c * rows, rows, False, half))

    for d in range(HALVES):
        c = sums[1].arrive(d)
        gather(full_c[0, c], oh_r)
        if d == HALVES - 1:
            exchanges[1].start(pair(fold_all(lambda e: fold(full_c[0, e] * full_c[0, e]))))
        if d < HALVES - 1:
            add_back(c * rows, rows, True)
    finish(sums[2], oh_c, lambda half: add_back(c * rows, rows, False, half))

    both = exchanges[0].total()
    norm0 = whole(both[:SUB])
    alpha0 = norm0 / (whole(exchanges[1].total()[:SUB]) + whole(both[SUB:]))

    for d in range(HALVES):
        c = sums[2].arrive(d)
        r1 = p0(c) - alpha0 * (full_r[1, c] + damp(c) * p0(c))
        r1_ref[c] = r1
        gather(r1, oh_c)
        if d == HALVES - 1:
            exchanges[2].start(pair(fold_all(lambda e: fold(r1_ref[e] * r1_ref[e]))))
        if d < HALVES - 1:
            add_forth(c * rows, rows, True)
    finish(sums[3], oh_r, lambda half: add_forth(c * rows, rows, False, half))

    norm1 = whole(exchanges[2].total()[:SUB])
    beta = norm1 / norm0

    def p1(c):
        return r1_ref[c] + beta * p0(c)

    def image1(c):
        return full_c[1, c] + beta * full_c[0, c]

    exchanges[4].start(pair(fold_all(lambda e: fold(p1(e) * damp(e) * p1(e)))))
    for d in range(HALVES):
        c = sums[3].arrive(d)
        gather(image1(c), oh_r)
        if d == HALVES - 1:
            exchanges[3].start(pair(fold_all(lambda e: fold(image1(e) * image1(e)))))
        if d < HALVES - 1:
            add_back(c * rows, rows, True)
    finish(sums[4], oh_c, lambda half: add_back(c * rows, rows, False, half))

    curv1 = whole(exchanges[3].total()[:SUB]) + whole(exchanges[4].total()[:SUB])
    alpha1 = norm1 / curv1
    for d in range(HALVES):
        c = sums[4].arrive(d)
        at = pl.ds(pl.multiple_of(c * rows, rows), rows)
        step_ref[at, :] = alpha0 * p0(c) + alpha1 * p1(c)
        out_ref[at, :] = r1_ref[c] - alpha1 * (full_r[2, c] + damp(c) * p1(c))

    for s in sums:
        s.drain()
    for e in exchanges:
        e.drain()


def on_device(n_row, n_col, jacobian, block_rows, block_cols, counts, residuals, damping):
    entries, _, slots = jacobian.shape[2:]
    res_width = residuals.shape[1]
    par_width = damping.shape[1]
    row = Group("row", n_row)
    col = Group("col", n_col)
    rows = entries // HALVES
    chips = n_col // 2
    n = max(n_row, n_col)
    vmem = pl.BlockSpec(memory_space=pltpu.VMEM)
    hbm = pl.BlockSpec(memory_space=pl.ANY)
    dma = pltpu.SemaphoreType.DMA
    out = jax.ShapeDtypeStruct((entries, par_width), F32)
    return pl.pallas_call(
        functools.partial(kernel, row, col),
        out_shape=(out, out),
        in_specs=[hbm, hbm, hbm, pl.BlockSpec(memory_space=pltpu.SMEM), hbm, hbm],
        out_specs=(vmem, vmem),
        scratch_shapes=[
            pltpu.VMEM((entries, entries, slots), BF16),
            pltpu.VMEM((1, slots), jnp.int32),
            pltpu.VMEM((1, slots), jnp.int32),
            pltpu.VMEM((entries, res_width), F32),
            pltpu.VMEM((entries, par_width), F32),
            pltpu.VMEM((res_width, slots), BF16),
            pltpu.VMEM((par_width, slots), BF16),
            pltpu.VMEM((rows, slots), F32),
            pltpu.VMEM((entries, slots), F32),
            pltpu.VMEM((entries, SUB, slots), F32),
            pltpu.VMEM((HALVES, rows, par_width), F32),
            pltpu.VMEM((3, HALVES, rows, par_width), F32),
            pltpu.VMEM((3, n_row, rows, par_width), F32),
            pltpu.VMEM((3, HALVES, rows, par_width), F32),
            pltpu.VMEM((2, HALVES, rows, res_width), F32),
            pltpu.VMEM((2, rows, res_width), F32),
            pltpu.VMEM((2, chips, rows, res_width), F32),
            pltpu.VMEM((2, HALVES, rows, res_width), F32),
            pltpu.VMEM((5, n, 2 * SUB, LANES), F32),
            dma((LOADS,)),
            dma((4,)),
            dma((3, HALVES, PIECES)),
            dma((3, n_row, PIECES)),
            dma((3, n_row, PIECES)),
            dma((3, HALVES, PIECES)),
            dma((2,)),
            dma((2,)),
            dma((2, chips)),
            dma((2, chips)),
            dma((2,)),
            dma((2,)),
            dma((5, n)),
            dma((5, n)),
        ],
        compiler_params=pltpu.CompilerParams(
            collective_id=0, has_side_effects=True, vmem_limit_bytes=48 * 1024 * 1024
        ),
        cost_estimate=pl.CostEstimate(
            flops=10 * entries * entries * slots,
            bytes_accessed=2 * entries * entries * slots,
            transcendentals=0,
        ),
        name="cg",
    )(
        jacobian.reshape(entries, entries, slots),
        block_rows.reshape(1, slots),
        block_cols.reshape(1, slots),
        counts,
        residuals,
        damping,
    )


def solution(mesh):
    placed = (
        P(("rig", "row"), "col", None, None, None),
        P(("rig", "row"), "col", None),
        P(("rig", "row"), "col", None),
        P(("rig", "row"), "col"),
        P(None, ("rig", "row")),
        P(None, ("rig", "col")),
    )
    return jax.shard_map(
        functools.partial(on_device, mesh.shape["row"], mesh.shape["col"]),
        mesh=mesh,
        in_specs=placed,
        out_specs=(P(None, ("rig", "col")), P(None, ("rig", "col"))),
        check_vma=False,
    )
```

time: 67 us -> 62.4 us (0.931)
  Pallas kernels: 61 us -> 56.4 us
    pallas_call x1, Pallas kernels: 61 us -> 56.4 us  [on_device(): pl.pallas_call(functools.partial(kernel, row, col), out_shape=(out, out),...]
where the time goes in v2:
time: 62.4 us; the launch traced here: 62.2 us
  Pallas kernels  56.4 us (90%)
  local copies, waits for them, and re-layouts  4.49 us (7%)
  between operations  1.3 us (2%)
    pallas_call x1, Pallas kernels, on_device(): pl.pallas_call(functools.partial(kernel, row, col), out_shape=(out, out),...  56.4 us
    unnamed x10, local copies, waits for them, and re-layouts  4.49 us

profile of v2, /device:TPU:0, one launch (start us, length us, event | category | flops | bytes accessed | tf_op | source)
XLA Modules:
  0.0 62.2 jit_solution(10476478174052667596)
XLA Ops:
  1.3 0.0 copy-start
  1.3 0.9 %copy-done = f32[64,512]{1,0:T(8,128)S(1)} copy-done((f32[64,512]{1,0:T(8,128)S(1)}, f32[64,512]{1,0:T(8,128)}, u32[]{:S(2)}) %copy-start) | copy-done | bytes 131096
  2.2 0.0 copy-start.1
  2.2 0.9 %copy-done.1 = f32[64,512]{1,0:T(8,128)S(1)} copy-done((f32[64,512]{1,0:T(8,128)S(1)}, f32[64,512]{1,0:T(8,128)}, u32[]{:S(2)}) %copy-start.1) | copy-done | bytes 131096
  3.1 0.0 copy-start.2
  3.1 0.7 %copy-done.2 = s32[1,1,1024]{2,1,0:T(1,128)S(1)} copy-done((s32[1,1,1024]{2,1,0:T(1,128)S(1)}, s32[1,1,1024]{2,1,0:T(1,128)}, u32[]{:S(2)}) %copy-start.2) | copy-done | bytes 4120
  3.8 0.0 copy-start.3
  3.8 0.7 %copy-done.3 = s32[1,1,1024]{2,1,0:T(1,128)S(1)} copy-done((s32[1,1,1024]{2,1,0:T(1,128)S(1)}, s32[1,1,1024]{2,1,0:T(1,128)}, u32[]{:S(2)}) %copy-start.3) | copy-done | bytes 4120
  4.5 56.4 %cg.1 = (f32[64,512]{1,0:T(8,128)S(1)}, f32[64,512]{1,0:T(8,128)S(1)}) custom-call(bf16[64,64,1024]{2,1,0:T(8,128)(2,1)} %bitcast.5, s32[1,1024]{1,0:T(1,128)S(1)} %bitcast.3, s32[1,1024]{1,0:T(1,128)S(1)} %bitcast.4, s32[1,1]{1,0:T(1,128)S(6)} %copy.10.count_ref, f32[64,512]{1,0:T(8,128)S(1)} %copy-done, f32[64,512]{1,0:T(8,128)S(1)} %copy-done.1), custom_call_target="tpu_custom_call" | custom-call | flops 41943040 | bytes 8388608 | tf_op jit(solution)/shard_map/cg/pallas_call | solution.py:469
  60.9 0.7 %copy.11 = f32[64,512]{1,0:T(8,128)} copy(f32[64,512]{1,0:T(8,128)S(1)} %get-tuple-element.4) | data formatting | bytes 262144
  61.5 0.7 %copy.12 = f32[64,512]{1,0:T(8,128)} copy(f32[64,512]{1,0:T(8,128)S(1)} %get-tuple-element.5) | data formatting | bytes 262144
Async XLA Ops:
  1.3 0.9 %copy-start = (f32[64,512]{1,0:T(8,128)S(1)}, f32[64,512]{1,0:T(8,128)}, u32[]{:S(2)}) copy-start(f32[64,512]{1,0:T(8,128)} %res_hbm.1) | copy-start | bytes 393220
  2.2 0.9 %copy-start.1 = (f32[64,512]{1,0:T(8,128)S(1)}, f32[64,512]{1,0:T(8,128)}, u32[]{:S(2)}) copy-start(f32[64,512]{1,0:T(8,128)} %damp_hbm.1) | copy-start | bytes 393220
  3.1 0.7 %copy-start.2 = (s32[1,1,1024]{2,1,0:T(1,128)S(1)}, s32[1,1,1024]{2,1,0:T(1,128)}, u32[]{:S(2)}) copy-start(s32[1,1,1024]{2,1,0:T(1,128)} %param.7) | copy-start | bytes 12292
  3.8 0.7 %copy-start.3 = (s32[1,1,1024]{2,1,0:T(1,128)S(1)}, s32[1,1,1024]{2,1,0:T(1,128)}, u32[]{:S(2)}) copy-start(s32[1,1,1024]{2,1,0:T(1,128)} %param.8) | copy-start | bytes 12292

commit v3 on v2

--- a/solution.py
+++ b/solution.py
@@ -327,14 +327,22 @@
         def body(kk, _):
             sl = pl.ds(pl.multiple_of(kk * LANES, LANES), LANES)
             g = g_ref[pl.ds(0, count), sl]
+            sums_here = []
             for a in range(width):
                 m = jac[a0 + a, pl.ds(b0, count), sl].astype(F32) * g
                 part = m[:SUB]
                 for r in range(SUB, count, SUB):
                     part = part + m[r : r + SUB]
-                acc3[a0 + a, :, sl] = part if first else acc3[a0 + a, :, sl] + part
-            if half is not None:
-                terms[pl.ds(a0, width), sl] = jnp.sum(acc3[pl.ds(a0, width), :, sl], axis=1)
+                if not first:
+                    part = part + acc3[a0 + a, :, sl]
+                if half is None:
+                    acc3[a0 + a, :, sl] = part
+                    continue
+                sums_here.append(part)
+                if len(sums_here) == SUB:
+                    at = pl.multiple_of(a0 + (a + 1 - SUB), SUB)
+                    terms[pl.ds(at, SUB), sl] = jnp.sum(jnp.stack(sums_here), axis=1)
+                    sums_here = []
             return 0
 
         lax.fori_loop(0, slots // LANES, body, 0)

time: 62.4 us -> 61.8 us (level)
    pallas_call x1, Pallas kernels: 56.4 us -> 55.8 us  [on_device(): pl.pallas_call(functools.partial(kernel, row, col), out_shape=(out, out),...]
where the time goes in v3:
time: 61.8 us; the launch traced here: 61.6 us
  Pallas kernels  55.8 us (90%)
  local copies, waits for them, and re-layouts  4.49 us (7%)
  between operations  1.3 us (2%)
    pallas_call x1, Pallas kernels, on_device(): pl.pallas_call(functools.partial(kernel, row, col), out_shape=(out, out),...  55.8 us
    unnamed x10, local copies, waits for them, and re-layouts  4.49 us

profile of v3, /device:TPU:0, one launch (start us, length us, event | category | flops | bytes accessed | tf_op | source)
XLA Modules:
  0.0 61.6 jit_solution(8225761239313384009)
XLA Ops:
  1.3 0.0 copy-start
  1.3 0.9 %copy-done = f32[64,512]{1,0:T(8,128)S(1)} copy-done((f32[64,512]{1,0:T(8,128)S(1)}, f32[64,512]{1,0:T(8,128)}, u32[]{:S(2)}) %copy-start) | copy-done | bytes 131096
  2.2 0.0 copy-start.1
  2.2 0.9 %copy-done.1 = f32[64,512]{1,0:T(8,128)S(1)} copy-done((f32[64,512]{1,0:T(8,128)S(1)}, f32[64,512]{1,0:T(8,128)}, u32[]{:S(2)}) %copy-start.1) | copy-done | bytes 131096
  3.1 0.0 copy-start.2
  3.1 0.7 %copy-done.2 = s32[1,1,1024]{2,1,0:T(1,128)S(1)} copy-done((s32[1,1,1024]{2,1,0:T(1,128)S(1)}, s32[1,1,1024]{2,1,0:T(1,128)}, u32[]{:S(2)}) %copy-start.2) | copy-done | bytes 4120
  3.8 0.0 copy-start.3
  3.8 0.7 %copy-done.3 = s32[1,1,1024]{2,1,0:T(1,128)S(1)} copy-done((s32[1,1,1024]{2,1,0:T(1,128)S(1)}, s32[1,1,1024]{2,1,0:T(1,128)}, u32[]{:S(2)}) %copy-start.3) | copy-done | bytes 4120
  4.5 55.8 %cg.1 = (f32[64,512]{1,0:T(8,128)S(1)}, f32[64,512]{1,0:T(8,128)S(1)}) custom-call(bf16[64,64,1024]{2,1,0:T(8,128)(2,1)} %bitcast.5, s32[1,1024]{1,0:T(1,128)S(1)} %bitcast.3, s32[1,1024]{1,0:T(1,128)S(1)} %bitcast.4, s32[1,1]{1,0:T(1,128)S(6)} %copy.10.count_ref, f32[64,512]{1,0:T(8,128)S(1)} %copy-done, f32[64,512]{1,0:T(8,128)S(1)} %copy-done.1), custom_call_target="tpu_custom_call" | custom-call | flops 41943040 | bytes 8388608 | tf_op jit(solution)/shard_map/cg/pallas_call | solution.py:477
  60.2 0.7 %copy.11 = f32[64,512]{1,0:T(8,128)} copy(f32[64,512]{1,0:T(8,128)S(1)} %get-tuple-element.4) | data formatting | bytes 262144
  60.9 0.7 %copy.12 = f32[64,512]{1,0:T(8,128)} copy(f32[64,512]{1,0:T(8,128)S(1)} %get-tuple-element.5) | data formatting | bytes 262144
Async XLA Ops:
  1.3 0.9 %copy-start = (f32[64,512]{1,0:T(8,128)S(1)}, f32[64,512]{1,0:T(8,128)}, u32[]{:S(2)}) copy-start(f32[64,512]{1,0:T(8,128)} %res_hbm.1) | copy-start | bytes 393220
  2.2 0.9 %copy-start.1 = (f32[64,512]{1,0:T(8,128)S(1)}, f32[64,512]{1,0:T(8,128)}, u32[]{:S(2)}) copy-start(f32[64,512]{1,0:T(8,128)} %damp_hbm.1) | copy-start | bytes 393220
  3.1 0.7 %copy-start.2 = (s32[1,1,1024]{2,1,0:T(1,128)S(1)}, s32[1,1,1024]{2,1,0:T(1,128)}, u32[]{:S(2)}) copy-start(s32[1,1,1024]{2,1,0:T(1,128)} %param.7) | copy-start | bytes 12292
  3.8 0.7 %copy-start.3 = (s32[1,1,1024]{2,1,0:T(1,128)S(1)}, s32[1,1,1024]{2,1,0:T(1,128)}, u32[]{:S(2)}) copy-start(s32[1,1,1024]{2,1,0:T(1,128)} %param.8) | copy-start | bytes 12292
